TPU v7x, 32 devices: a whole 2x2x4 slice. The times are simulated.
32 devices in a mesh: dp: 32 (over z, y, x, core).
Axes of the slice: x: 2, y: 2, z: 4, core: 2. Of those that a mesh axis runs over, the one named last changes fastest.
Arguments:
- inputs: bfloat16 [31520, 384], P('dp'), may hold values from -6 to 6
- weights: bfloat16 [13824, 128], P('dp'), may hold values from -0.8164966 to 0.8164966
- vectors: float32 [36, 128], replicated, may hold values from -2 to 2
- cotangent: bfloat16 [31520, 384], P('dp'), may hold values from -6 to 6
- mom_weights: float32 [13824, 128], P('dp'), may hold values from -213.046474 to 213.046474
- mom_vectors: float32 [36, 128], replicated, may hold values from -355.07746 to 355.07746
Outputs:
- output: bfloat16 [31520, 384], P('dp')
- grad_inputs: float32 [31520, 384], P('dp')
- grad_weights: float32 [13824, 128], P('dp')
- grad_vectors: float32 [36, 128], replicated
- new_mom_weights: float32 [13824, 128], P('dp')
- new_mom_vectors: float32 [36, 128], replicated
- update_weights: float32 [13824, 128], P('dp')
- update_vectors: float32 [36, 128], replicated
All inputs are finite; a program needn't handle non-finite values.
Results may differ from a plain program's by a relative error of at most 0.012.
Values may be sent and summed in bfloat16 or wider, within the bound.
A program may use at most 128 MiB of HBM per device.

v0:
```python
import math

import jax
import jax.numpy as jnp
from jax import lax
from jax.sharding import PartitionSpec as P

D = 384
HEADS = 6
HD = 64
FF = 1536
SEQ = 197


HIGH = lax.Precision.HIGHEST
MOMENTUM = 0.95
MATRIX_RATE = 0.5
VECTOR_RATE = 0.2
NEWTON_COEFFS = (3.4445, -4.775, 2.0315)
NORM_EPS = 1e-06


def split_matrices(flat):
    flat_line = flat.reshape(-1)
    layout = ((D, 3 * D), (D, D), (D, FF), (FF, D))
    pieces = []
    offset = 0
    for dims_pair in layout:
        entries = dims_pair[0] * dims_pair[1]
        pieces.append(flat_line[offset : offset + entries].reshape(dims_pair))
        offset = offset + entries
    return pieces


def split_vectors(flat):
    flat_line = flat.reshape(-1)
    pieces = []
    offset = 0
    for length_one in (D, D, D, D, D, D, D, D, FF):
        pieces.append(flat_line[offset : offset + length_one])
        offset = offset + length_one
    return pieces


def layer_norm(value, norm_gain, norm_shift):
    center = jnp.mean(value, axis=-1, keepdims=True)
    deviation = value - center
    spread = jnp.mean(deviation * deviation, axis=-1, keepdims=True)
    return deviation * lax.rsqrt(spread + NORM_EPS) * norm_gain + norm_shift


def gelu_exact(value):
    return jax.nn.gelu(value, approximate=False)


def matmul(left, right):
    return jnp.dot(left, right, preferred_element_type=jnp.float32)


def outer_sum(left, right):
    return lax.dot_general(
        left, right, (((0,), (0,)), ((), ())), preferred_element_type=jnp.float32
    )


def times_transpose(left, right):
    return lax.dot_general(
        left, right, (((1,), (1,)), ((), ())), preferred_element_type=jnp.float32
    )


def column_sums(value):
    return jnp.sum(value.astype(jnp.float32), axis=0)


def orthogonalize(matrix):
    tall = matrix.shape[0] > matrix.shape[1]
    current = matrix.T if tall else matrix
    current = current / (jnp.sqrt(jnp.sum(current * current)) + 1e-07)
    first, second, third = NEWTON_COEFFS
    for repeat in range(5):
        square = jnp.dot(current, current.T, precision=HIGH)
        poly = second * square + third * jnp.dot(square, square, precision=HIGH)
        current = first * current + jnp.dot(poly, current, precision=HIGH)
    return current.T if tall else current


def blank_like(matrix):
    return jnp.zeros_like(matrix)


def on_device(inputs, weights, vectors, cotangent, mom_weights, mom_vectors):
    count = lax.axis_size("dp")
    device_index = lax.axis_index("dp")
    whole = lax.all_gather(weights, "dp", axis=0, tiled=True)
    w_qkv, w_out, w_up, w_down = split_matrices(whole)
    ln1_gain, ln1_shift, bias_q, bias_v, bias_out, ln2_gain, ln2_shift, bias_down, bias_up = (
        split_vectors(vectors)
    )
    rows = inputs.shape[0]
    images = rows // SEQ
    scale_qk = HD ** (-0.5)
    residual_in = inputs.astype(jnp.float32)
    normed, norm_pull = jax.vjp(layer_norm, residual_in, ln1_gain, ln1_shift)
    normed_low = normed.astype(jnp.bfloat16)
    bias_qkv = jnp.concatenate([bias_q, jnp.zeros_like(bias_q), bias_v])
    qkv = (
        (matmul(normed_low, w_qkv) + bias_qkv)
        .astype(jnp.bfloat16)
        .reshape(images, SEQ, 3, HEADS, HD)
    )
    queries = qkv[:, :, 0]
    key_rows = qkv[:, :, 1]
    values = qkv[:, :, 2]
    scores = (
        jnp.einsum("bqhd,bkhd->bhqk", queries, key_rows, preferred_element_type=jnp.float32)
        * scale_qk
    )
    row_max = jnp.max(scores, axis=-1, keepdims=True)
    log_total = row_max + jnp.log(jnp.sum(jnp.exp(scores - row_max), axis=-1, keepdims=True))
    probs_low = jnp.exp(scores - log_total).astype(jnp.bfloat16)
    attended = jnp.einsum("bhqk,bkhd->bqhd", probs_low, values, preferred_element_type=jnp.float32)
    attended = attended.reshape(rows, D).astype(jnp.bfloat16)
    middle = residual_in + matmul(attended, w_out) + bias_out
    normed_two, norm_pull_two = jax.vjp(layer_norm, middle, ln2_gain, ln2_shift)
    normed_two_low = normed_two.astype(jnp.bfloat16)
    hidden = matmul(normed_two_low, w_up) + bias_up
    unused_out, gelu_pull = jax.vjp(gelu_exact, hidden)
    active = gelu_exact(hidden).astype(jnp.bfloat16)
    result = middle + matmul(active, w_down) + bias_down
    output = result.astype(jnp.bfloat16)
    again = lax.all_gather(weights, "dp", axis=0, tiled=True)
    w_qkv, w_out, w_up, w_down = split_matrices(again)
    grad_down = outer_sum(active, cotangent)
    grad_bias_down = column_sums(cotangent)
    d_active = times_transpose(cotangent, w_down)
    d_hidden = gelu_pull(d_active)[0].astype(jnp.bfloat16)
    grad_up = outer_sum(normed_two_low, d_hidden)
    grad_bias_up = column_sums(d_hidden)
    d_normed_two = times_transpose(d_hidden, w_up)
    d_middle_norm, grad_ln2_gain, grad_ln2_shift = norm_pull_two(d_normed_two)
    d_middle = cotangent.astype(jnp.float32) + d_middle_norm
    d_branch = d_middle.astype(jnp.bfloat16)
    grad_out = outer_sum(attended, d_branch)
    grad_bias_out = column_sums(d_branch)
    d_attended = (
        times_transpose(d_branch, w_out).astype(jnp.bfloat16).reshape(images, SEQ, HEADS, HD)
    )
    scores_again = (
        jnp.einsum("bqhd,bkhd->bhqk", queries, key_rows, preferred_element_type=jnp.float32)
        * scale_qk
    )
    probs_full = jnp.exp(scores_again - log_total)
    probs_again = probs_full.astype(jnp.bfloat16)
    grad_values = jnp.einsum(
        "bhqk,bqhd->bkhd", probs_again, d_attended, preferred_element_type=jnp.float32
    )
    d_probs = jnp.einsum("bqhd,bkhd->bhqk", d_attended, values, preferred_element_type=jnp.float32)
    d_scores = probs_full * (d_probs - jnp.sum(d_probs * probs_full, axis=-1, keepdims=True))
    d_scores = d_scores.astype(jnp.bfloat16)
    grad_queries = (
        jnp.einsum("bhqk,bkhd->bqhd", d_scores, key_rows, preferred_element_type=jnp.float32)
        * scale_qk
    )
    grad_keys = (
        jnp.einsum("bhqk,bqhd->bkhd", d_scores, queries, preferred_element_type=jnp.float32)
        * scale_qk
    )
    d_qkv = (
        jnp.stack([grad_queries, grad_keys, grad_values], axis=2)
        .astype(jnp.bfloat16)
        .reshape(rows, 3 * D)
    )
    grad_qkv = outer_sum(normed_low, d_qkv)
    grad_bias_q = column_sums(d_qkv[:, :D])
    grad_bias_v = column_sums(d_qkv[:, 2 * D :])
    d_normed = times_transpose(d_qkv, w_qkv)
    d_input_norm, grad_ln1_gain, grad_ln1_shift = norm_pull(d_normed)
    grad_inputs = d_middle + d_input_norm
    local_grads = jnp.concatenate(
        [grad_qkv.reshape(-1), grad_out.reshape(-1), grad_up.reshape(-1), grad_down.reshape(-1)]
    )
    local_grads = local_grads.reshape(-1, 128)
    local_vector_grads = jnp.concatenate(
        [
            grad_ln1_gain,
            grad_ln1_shift,
            grad_bias_q,
            grad_bias_v,
            grad_bias_out,
            grad_ln2_gain,
            grad_ln2_shift,
            grad_bias_down,
            grad_bias_up,
        ]
    ).reshape(-1, 128)
    grad_vectors = lax.psum(local_vector_grads, "dp")
    grad_weights = lax.psum_scatter(local_grads, "dp", scatter_dimension=0, tiled=True)
    new_mom_weights = MOMENTUM * mom_weights + grad_weights
    gathered = lax.all_gather(new_mom_weights, "dp", axis=0, tiled=True)
    new_mom_vectors = MOMENTUM * mom_vectors + grad_vectors
    mom_matrices = split_matrices(gathered)
    owned_list = []
    for matrix_slot in range(4):
        owner_rank = 0
        computed = lax.cond(
            device_index == owner_rank, orthogonalize, blank_like, mom_matrices[matrix_slot]
        )
        owned_list.append(computed)
    owned_flat = jnp.concatenate([item.reshape(-1) for item in owned_list]).reshape(-1, 128)
    own_rows = lax.psum_scatter(owned_flat, "dp", scatter_dimension=0, tiled=True)
    update_weights = -MATRIX_RATE * own_rows
    total_tokens = rows * count
    update_vectors = -(VECTOR_RATE / math.sqrt(total_tokens)) * new_mom_vectors
    return (
        output,
        grad_inputs,
        grad_weights,
        grad_vectors,
        new_mom_weights,
        new_mom_vectors,
        update_weights,
        update_vectors,
    )


def solution(mesh):
    in_specs = (P("dp", None), P("dp", None), P(), P("dp", None), P("dp", None), P())
    out_specs = (
        P("dp", None),
        P("dp", None),
        P("dp", None),
        P(),
        P("dp", None),
        P(),
        P("dp", None),
        P(),
    )
    return jax.shard_map(
        on_device, mesh=mesh, in_specs=in_specs, out_specs=out_specs, check_vma=False
    )
```

profile of v0, /device:TPU:21, one launch (start us, length us, event | category | flops | bytes accessed | tf_op | source)
XLA Modules:
  0.0 738.9 jit_solution(9406631774744465408)
XLA Ops:
  11.3 1.5 fusion.50
  14.8 56.4 %all-gather.3.cloned.1.call-done = bf16[13824,128]{1,0:T(8,128)(2,1)} async-done(((bf16[432,128]{1,0:T(8,128)(2,1)}), bf16[13824,128]{1,0:T(8,128)(2,1)}) %all-gather.3.cloned.1.call-update) | async-done | bytes 3538960 | tf_op jit(solution)/shard_map/all_gather | solution.py:95
  72.4 1.9 reshape.249
  74.3 1.8 fusion.80
  77.6 2.2 reshape.252
  79.7 2.7 fusion.40
  82.4 5.7 reshape.262
  88.2 5.8 fusion.79
  93.9 3.3 copy.51
  97.3 4.1 copy.50
  101.4 3.8 copy.52
  113.5 15.7 %multiply_convert_fusion.1 = (bf16[985,1536]{1,0:T(8,128)(2,1)}, f32[985,1536]{1,0:T(8,128)S(1)}, f32[985,1536]{1,0:T(8,128)S(1)}) fusion(f32[1536]{0:T(1024)S(1)} %copy-done.31, bf16[384,1536]{1,0:T(8,128)(2,1)S(1)} %copy-done.24, f32[985,384]{1,0:T(8,128)S(1)} %get-tuple-element.75, f32[384]{0:T(512)S(1)} %copy-done.36, f32[384]{0:T(512)S(1)} %get-tuple-element.66, ...), kind=kOutput, calls=%fused_computation.96 | convolution fusion | flops 1263699840 | bytes 17839304 | tf_op jit(solution)/shard_map/dot_general | solution.py:57
  129.2 3.8 convert_reduce_fusion
  133.0 2.1 multiply_reduce_fusion.6
  135.0 3.0 fusion.73
  141.0 2.5 reshape.263
  143.5 3.8 copy.35
  147.4 5.4 convolution_bitcast_fusion
  152.8 2.1 multiply_reduce_fusion.4
  154.9 2.1 multiply_convert_fusion
  157.0 2.1 multiply_bitcast_fusion
  159.1 1.7 multiply_bitcast_fusion.1
  161.6 3.2 fusion.102
  164.8 2.3 reshape.258
  167.2 3.1 reshape.257
  170.3 1.9 reshape.256
  172.2 2.5 maximum_convert_fusion
  174.7 4.5 copy.40
  179.2 7.6 %convert_element_type.97 = bf16[985,1152]{0,1:T(8,128)(2,1)} reshape(bf16[5,197,3,6,64]{1,0,4,3,2:T(8,128)(2,1)} %copy.40) | data formatting | bytes 4538880 | tf_op jit(solution)/shard_map/convert_element_type | solution.py:171
  186.7 4.5 fusion.69
  191.2 2.5 reshape.255
  193.7 8.9 %maximum_bitcast_fusion = f32[13824,128]{1,0:T(8,128)} fusion(f32[589824]{0:T(1024)S(1)} %reshape.258, f32[589824]{0:T(1024)} %reshape.257, f32[147456]{0:T(1024)} %reshape.256, f32[442368]{0:T(1024)} %reshape.255), kind=kLoop, calls=%fused_computation.87 | loop fusion | flops 5308416 | bytes 14155776 | tf_op jit(solution)/shard_map/reshape | solution.py:183
  202.7 116.4 %reduce-scatter.3.cloned.1.call-done = f32[432,128]{1,0:T(8,128)} async-done(((f32[13824,128]{1,0:T(8,128)}), f32[432,128]{1,0:T(8,128)}) %reduce-scatter.3.cloned.1.call-update) | async-done | bytes 221200 | tf_op jit(solution)/shard_map/reduce_scatter | solution.py:198
  319.1 1.6 multiply_add_fusion.9
  320.8 76.2 %all-gather.5.cloned.1.call-done = f32[13824,128]{1,0:T(8,128)} async-done(((f32[432,128]{1,0:T(8,128)}), f32[13824,128]{1,0:T(8,128)}) %all-gather.5.cloned.1.call-update) | async-done | bytes 7077904 | tf_op jit(solution)/shard_map/all_gather | solution.py:200
  397.1 9.5 %conditional.5 = (f32[147456]{0:T(1024)S(1)}) conditional(s32[]{:T(128)} %convert_element_type.102, () %tuple.41, f32[13824,128]{1,0:T(8,128)} %all-gather.5.cloned.1.call-done), branch_computations={%region_25.0_spmd, %region_26.28_spmd} | conditional | flops 10196287488 | bytes 24772644 | solution.py:206
  407.4 16.1 %conditional.4 = (f32[442368]{0:T(1024)S(1)}) conditional(s32[]{:T(128)} %convert_element_type.102, () %tuple.40, f32[13824,128]{1,0:T(8,128)} %all-gather.5.cloned.1.call-done), branch_computations={%region_22.0_spmd, %region_23.25_spmd} | conditional | flops 23789666304 | bytes 50724900 | solution.py:206
  424.7 18.2 %conditional.7 = (f32[589824]{0:T(1024)S(1)}) conditional(s32[]{:T(128)} %convert_element_type.102, () %tuple.43, f32[13824,128]{1,0:T(8,128)} %all-gather.5.cloned.1.call-done), branch_computations={%region_31.32_spmd, %region_32.34_spmd} | conditional | flops 30598152192 | bytes 141557856 | solution.py:206
  444.3 13.0 %conditional.6 = (f32[589824]{0:T(1024)}) conditional(s32[]{:T(128)} %convert_element_type.102, () %tuple.42, f32[13824,128]{1,0:T(8,128)} %all-gather.5.cloned.1.call-done), branch_computations={%region_28.0_spmd, %region_29.31_spmd} | conditional | flops 30586355712 | bytes 63701028 | solution.py:206
  444.3 1.5 reshape.232
  457.3 7.3 maximum_bitcast_fusion.1
  464.6 1.6 copy-done.18
  466.3 3.0 fusion.75
  470.9 1.8 convert_reduce_fusion.2
  472.7 187.4 %psum.7 = f32[36,128]{1,0:T(8,128)S(1)} all-reduce(f32[36,128]{1,0:T(8,128)S(1)} %bitcast.231), channel_id=1, replica_groups=mesh['dp'=32] {'dp'}, use_global_device_ids=true, to_apply=%region_21.0 | all-reduce | flops 4608 | bytes 36864 | tf_op jit(solution)/shard_map/psum | solution.py:197
  660.8 4.8 add_convert_fusion.1
  665.6 64.9 %reduce-scatter.5.cloned.1.call-done = f32[432,128]{1,0:T(8,128)} async-done(((f32[13824,128]{1,0:T(8,128)}), f32[432,128]{1,0:T(8,128)}) %reduce-scatter.5.cloned.1.call-update) | async-done | bytes 221200 | tf_op jit(solution)/shard_map/reduce_scatter | solution.py:211
  730.5 1.6 broadcast_multiply_fusion.1
  (128 shorter events, 26.7 us)
Async XLA Ops:
  7.2 64.0 %all-gather.3.cloned.1.call-start = ((), (), s32[]{:S(2)}) async-start(), calls=%async_computation.2 | async-start | bytes 3649536 | tf_op jit(solution)/shard_map/all_gather | solution.py:95
  7.9 311.2 %reduce-scatter.3.cloned.1.call-start = ((), (), s32[]{:S(2)}) async-start(), calls=%async_computation.3 | async-start | bytes 7299072 | tf_op jit(solution)/shard_map/reduce_scatter | solution.py:198
  12.9 0.6 copy-start.27
  71.1 1.3 slice-start.2
  76.1 3.6 copy-start.3
  76.1 3.6 copy-start.30
  76.1 3.6 copy-start.34
  97.3 7.9 %copy-start.10 = (bf16[5,197,1,6,64]{1,4,3,0,2:T(8,128)(2,1)}, bf16[5,197,1,6,64]{1,4,3,0,2:T(8,128)(2,1)S(1)}, u32[]{:S(2)}) copy-start(bf16[5,197,1,6,64]{1,4,3,0,2:T(8,128)(2,1)S(1)} %copy.51) | copy-start | bytes 2269444
  105.2 1.1 copy-start.12
  106.3 2.6 copy-start
  106.3 2.6 copy-start.14
  110.2 2.0 copy-start.32
  112.1 1.3 copy-start.24
  112.2 1.3 copy-start.31
  112.2 1.3 copy-start.36
  113.0 25.0 %copy-start.4 = (f32[985,384]{1,0:T(8,128)}, f32[985,384]{1,0:T(8,128)S(1)}, u32[]{:S(2)}) copy-start(f32[985,384]{1,0:T(8,128)S(1)} %get-tuple-element.75) | copy-start | bytes 4538884
  113.4 15.7 %copy-start.19 = (bf16[985,384]{1,0:T(8,128)(2,1)S(1)}, bf16[985,384]{1,0:T(8,128)(2,1)}, u32[]{:S(2)}) copy-start(bf16[985,384]{1,0:T(8,128)(2,1)} %param.17) | copy-start | bytes 2269444
  113.4 15.7 %copy-start.23 = (bf16[1536,384]{1,0:T(8,128)(2,1)S(1)}, bf16[1536,384]{1,0:T(8,128)(2,1)}, u32[]{:S(2)}) copy-start(bf16[1536,384]{1,0:T(8,128)(2,1)} %reshape.253) | copy-start | bytes 3538948
  138.7 1.7 copy-start.6
  143.5 9.2 %slice-start = ((s8[6144000]{0:T(1024)(128)(4,1)}), s8[1949696]{0:T(1024)(128)(4,1)S(1)}, s32[]{:S(2)}) async-start(s8[6144000]{0:T(1024)(128)(4,1)} %bitcast.229), calls=%async_computation.6 | async-start | bytes 3899392
  147.4 5.4 slice-start.1
  147.4 5.4 copy-start.15
  147.4 5.4 copy-start.16
  154.9 2.1 copy-start.11
  157.0 2.1 copy-start.13
  159.1 1.7 copy-start.20
  159.1 2.5 copy-start.37
  179.2 7.6 %copy-start.35 = (f32[384]{0:T(512)S(1)}, f32[384]{0:T(512)}, u32[]{:S(2)}) copy-start(f32[384]{0:T(512)} %get-tuple-element.70) | copy-start | bytes 4612
  202.6 116.5 %copy-start.25 = (f32[432,128]{1,0:T(8,128)S(1)}, f32[432,128]{1,0:T(8,128)}, u32[]{:S(2)}) copy-start(f32[432,128]{1,0:T(8,128)} %param.18) | copy-start | bytes 663556
  202.6 194.4 %all-gather.5.cloned.1.call-start = ((), (), s32[]{:S(2)}) async-start(), calls=%async_computation.4 | async-start | bytes 7299072 | tf_op jit(solution)/shard_map/all_gather | solution.py:200
  320.8 409.7 %reduce-scatter.5.cloned.1.call-start = ((), (), s32[]{:S(2)}) async-start(), calls=%async_computation.5 | async-start | bytes 7299072 | tf_op jit(solution)/shard_map/reduce_scatter | solution.py:211
  406.6 0.8 copy-start.22
  423.5 1.2 copy-start.17
  442.9 1.4 copy-start.8
  464.6 1.7 copy-start.18
  466.2 3.0 copy-start.28
  469.3 1.4 copy-start.7
  469.3 1.6 copy-start.21
  470.8 189.3 %copy-start.29 = (f32[36,128]{1,0:T(8,128)S(1)}, f32[36,128]{1,0:T(8,128)}, u32[]{:S(2)}) copy-start(f32[36,128]{1,0:T(8,128)} %param.19) | copy-start | bytes 55300
  470.8 189.9 %copy-start.5 = (f32[985,384]{1,0:T(8,128)S(1)}, f32[985,384]{1,0:T(8,128)}, u32[]{:S(2)}) copy-start(f32[985,384]{1,0:T(8,128)} %copy-done.4) | copy-start | bytes 4538884
  470.8 189.9 %copy-start.33 = (f32[384]{0:T(512)S(1)}, f32[384]{0:T(512)}, u32[]{:S(2)}) copy-start(f32[384]{0:T(512)} %get-tuple-element.64) | copy-start | bytes 4612
  660.1 5.5 copy-start.26
Sparse Core Ops, SparseCore 0:
  10.9 60.1 all-gather.2
  202.7 116.3 reduce-scatter.2
  323.0 74.0 all-gather.4
  464.7 265.7 reduce-scatter.4
where the time goes:
time: 752 us; the launch traced here: 739 us
  waiting for transfers between devices  315 us (42%)
  blocking collectives  187 us (25%)
  local copies, waits for them, and re-layouts  74.4 us (10%)
  matrix products  59.2 us (8%)
  loops' own time  54.9 us (7%)
  other arithmetic  33.6 us (4%)
  between operations  14.5 us (2%)
    psum x1, blocking collectives, on_device(): grad_vectors = lax.psum(local_vector_grads, 'dp')  187 us
    reduce_scatter x1, waiting for transfers between devices, on_device(): lax.psum_scatter(local_grads, 'dp', scatter_dimension=0, tiled=True)  116 us
    all_gather x1, waiting for transfers between devices, on_device(): gathered = lax.all_gather(new_mom_weights, 'dp', axis=0, tiled=True)  76.2 us
    reduce_scatter x1, waiting for transfers between devices, on_device(): lax.psum_scatter(owned_flat, 'dp', scatter_dimension=0, tiled=True)  64.9 us
    all_gather x1, waiting for transfers between devices, on_device(): whole = lax.all_gather(weights, 'dp', axis=0, tiled=True)  56.4 us
    another operation x4, loops' own time, on_device(): lax.cond(device_index == owner_rank, orthogonalize, blank_like, mom_matri...  54.9 us
    dot_general x4, matrix products, matmul(): return jnp.dot(left, right, preferred_element_type=jnp.float32)  24 us
    unnamed x85, local copies, waits for them, and re-layouts  19.5 us
  transfers between devices with their start and end apart: 4, of which 4 were waited for; matrix products, arithmetic and copies ran while one was open for 2% of the time, Pallas kernels for 0%

commit v1 on v0

--- a/solution.py
+++ b/solution.py
@@ -1,8 +1,11 @@
+import functools
 import math
 
 import jax
 import jax.numpy as jnp
 from jax import lax
+from jax.experimental import pallas as pl
+from jax.experimental.pallas import tpu as pltpu
 from jax.sharding import PartitionSpec as P
 
 D = 384
@@ -73,25 +76,102 @@
     return jnp.sum(value.astype(jnp.float32), axis=0)
 
 
-def orthogonalize(matrix):
-    tall = matrix.shape[0] > matrix.shape[1]
-    current = matrix.T if tall else matrix
-    current = current / (jnp.sqrt(jnp.sum(current * current)) + 1e-07)
+EDGES = (0, 3 * D * D // 128, 4 * D * D // 128, (4 * D * D + D * FF) // 128, (4 * D * D + 2 * D * FF) // 128)
+WIDTHS = (3 * D // 128, D // 128, FF // 128, D // 128)
+
+
+def split_low(value):
+    high = value.astype(jnp.bfloat16)
+    return high, (value - high.astype(jnp.float32)).astype(jnp.bfloat16)
+
+
+def dot_split(left, right, dims=((1,), (0,))):
+    def one(a, b):
+        return lax.dot_general(a, b, (dims, ((), ())), preferred_element_type=jnp.float32)
+
+    return one(left[0], right[0]) + (one(left[0], right[1]) + one(left[1], right[0]))
+
+
+def polar_kernel(rows, mom_ref, out_ref, flat, x_high, x_low, gram, poly_total):
+    first_row = lax.axis_index("dp") * rows
     first, second, third = NEWTON_COEFFS
-    for repeat in range(5):
-        square = jnp.dot(current, current.T, precision=HIGH)
-        poly = second * square + third * jnp.dot(square, square, precision=HIGH)
-        current = first * current + jnp.dot(poly, current, precision=HIGH)
-    return current.T if tall else current
-
-
-def blank_like(matrix):
-    return jnp.zeros_like(matrix)
+    eye = (
+        lax.broadcasted_iota(jnp.int32, (D, D), 0) == lax.broadcasted_iota(jnp.int32, (D, D), 1)
+    ).astype(jnp.float32)
+
+    def run(slot):
+        low_edge, high_edge, width = EDGES[slot], EDGES[slot + 1], WIDTHS[slot]
+        height = (high_edge - low_edge) // width
+        tall = height > D
+        wide = height if tall else width * 128
+        total = jnp.zeros((1, 128), jnp.float32)
+        for block in range(width):
+            piece = mom_ref[pl.ds(low_edge + block, height, stride=width), :]
+            total = total + jnp.sum(piece * piece, axis=0, keepdims=True)
+            if tall:
+                piece = piece.T
+                at = (slice(block * 128, block * 128 + 128), slice(0, height))
+            else:
+                at = (slice(0, height), slice(block * 128, block * 128 + 128))
+            high, low = split_low(piece)
+            x_high[at] = high
+            x_low[at] = low
+        norm = jnp.sqrt(jnp.sum(total)) + 1e-07
+        inverse = 1.0 / norm
+        whole = (x_high[:, :wide], x_low[:, :wide])
+        gram[...] = dot_split(whole, whole, ((1,), (1,))) * (inverse * inverse)
+        poly_total[...] = eye
+
+        def step(_, carry):
+            square = gram[...]
+            square_parts = split_low(square)
+            poly = first * eye + second * square + third * dot_split(square_parts, square_parts)
+            poly_parts = split_low(poly)
+            poly_total[...] = dot_split(poly_parts, split_low(poly_total[...]))
+            half = dot_split(poly_parts, square_parts)
+            gram[...] = dot_split(split_low(half), poly_parts)
+            return carry
+
+        lax.fori_loop(0, 5, step, 0)
+        total_parts = split_low(poly_total[...] * (inverse * -MATRIX_RATE))
+        for block in range(width):
+            if tall:
+                lines = slice(block * 128, block * 128 + 128)
+                some = (total_parts[0][lines], total_parts[1][lines])
+                done = dot_split(some, (x_high[:, :wide], x_low[:, :wide])).T
+            else:
+                lines = slice(block * 128, block * 128 + 128)
+                done = dot_split(total_parts, (x_high[:, lines], x_low[:, lines]))
+            flat[pl.ds(low_edge + block, height, stride=width), :] = done
+
+    for slot in range(4):
+        needed = jnp.logical_and(
+            first_row < EDGES[slot + 1], first_row + rows > EDGES[slot]
+        )
+        pl.when(needed)(lambda slot=slot: run(slot))
+    out_ref[...] = flat[pl.ds(first_row, rows), :]
+
+
+def polar_update(mom, rows):
+    return pl.pallas_call(
+        functools.partial(polar_kernel, rows),
+        out_shape=jax.ShapeDtypeStruct((rows, 128), jnp.float32),
+        in_specs=[pl.BlockSpec(memory_space=pltpu.VMEM)],
+        out_specs=pl.BlockSpec(memory_space=pltpu.VMEM),
+        scratch_shapes=[
+            pltpu.VMEM(mom.shape, jnp.float32),
+            pltpu.VMEM((D, FF), jnp.bfloat16),
+            pltpu.VMEM((D, FF), jnp.bfloat16),
+            pltpu.VMEM((D, D), jnp.float32),
+            pltpu.VMEM((D, D), jnp.float32),
+        ],
+        compiler_params=pltpu.CompilerParams(vmem_limit_bytes=48 * 1024 * 1024),
+        name="polar",
+    )(mom)
 
 
 def on_device(inputs, weights, vectors, cotangent, mom_weights, mom_vectors):
     count = lax.axis_size("dp")
-    device_index = lax.axis_index("dp")
     whole = lax.all_gather(weights, "dp", axis=0, tiled=True)
     w_qkv, w_out, w_up, w_down = split_matrices(whole)
     ln1_gain, ln1_shift, bias_q, bias_v, bias_out, ln2_gain, ln2_shift, bias_down, bias_up = (
@@ -194,22 +274,12 @@
             grad_bias_up,
         ]
     ).reshape(-1, 128)
-    grad_vectors = lax.psum(local_vector_grads, "dp")
+    grad_vectors = jnp.sum(lax.all_gather(local_vector_grads, "dp"), axis=0)
     grad_weights = lax.psum_scatter(local_grads, "dp", scatter_dimension=0, tiled=True)
     new_mom_weights = MOMENTUM * mom_weights + grad_weights
     gathered = lax.all_gather(new_mom_weights, "dp", axis=0, tiled=True)
     new_mom_vectors = MOMENTUM * mom_vectors + grad_vectors
-    mom_matrices = split_matrices(gathered)
-    owned_list = []
-    for matrix_slot in range(4):
-        owner_rank = 0
-        computed = lax.cond(
-            device_index == owner_rank, orthogonalize, blank_like, mom_matrices[matrix_slot]
-        )
-        owned_list.append(computed)
-    owned_flat = jnp.concatenate([item.reshape(-1) for item in owned_list]).reshape(-1, 128)
-    own_rows = lax.psum_scatter(owned_flat, "dp", scatter_dimension=0, tiled=True)
-    update_weights = -MATRIX_RATE * own_rows
+    update_weights = polar_update(gathered, mom_weights.shape[0])
     total_tokens = rows * count
     update_vectors = -(VECTOR_RATE / math.sqrt(total_tokens)) * new_mom_vectors
     return (

time: 752 us -> 467 us (0.62)
  blocking collectives: 187 us -> 35.8 us
  waiting for transfers between devices: 315 us -> 205 us
  loops' own time: 54.9 us -> 0 us
  Pallas kernels: 0 us -> 40.4 us
  other arithmetic: 33.6 us -> 22.3 us
    psum x1 -> x0, blocking collectives: 187 us -> none  [on_device(): grad_vectors = lax.psum(local_vector_grads, 'dp')]
    reduce_scatter x1 -> x0, waiting for transfers between devices: 64.9 us -> none  [on_device(): lax.psum_scatter(owned_flat, 'dp', scatter_dimension=0, tiled=True)]
    another operation x4 -> x0, loops' own time: 54.9 us -> none  [on_device(): lax.cond(device_index == owner_rank, orthogonalize, blank_like, mom_matri...]
    all_gather x1, waiting for transfers between devices: 76.2 us -> 30.3 us  [on_device(): gathered = lax.all_gather(new_mom_weights, 'dp', axis=0, tiled=True)]
    pallas_call x0 -> x1, Pallas kernels: none -> 40.4 us  [polar_update(): pl.pallas_call(functools.partial(polar_kernel, rows), out_shape=jax.Shape...]
    all_gather x0 -> x1, blocking collectives: none -> 35.8 us  [on_device(): grad_vectors = jnp.sum(lax.all_gather(local_vector_grads, 'dp'), axis=0)]
    unnamed x85 -> x109, local copies, waits for them, and re-layouts: 19.5 us -> 16.3 us
  transfers between devices with their start and end apart: 4 -> 3, of which waited for: 4 -> 3; matrix products, arithmetic and copies ran while one was open for 2% -> 4% of each run, Pallas kernels for 0% -> 0%
where the time goes in v1:
time: 467 us; the launch traced here: 460 us
  waiting for transfers between devices  205 us (44%)
  local copies, waits for them, and re-layouts  76.4 us (16%)
  matrix products  64.9 us (14%)
  Pallas kernels  40.4 us (9%)
  blocking collectives  35.8 us (8%)
  other arithmetic  22.3 us (5%)
  between operations  14.6 us (3%)
    reduce_scatter x1, waiting for transfers between devices, on_device(): lax.psum_scatter(local_grads, 'dp', scatter_dimension=0, tiled=True)  117 us
    all_gather x1, waiting for transfers between devices, on_device(): whole = lax.all_gather(weights, 'dp', axis=0, tiled=True)  57.5 us
    pallas_call x1, Pallas kernels, polar_update(): pl.pallas_call(functools.partial(polar_kernel, rows), out_shape=jax.Shape...  40.4 us
    all_gather x1, blocking collectives, on_device(): grad_vectors = jnp.sum(lax.all_gather(local_vector_grads, 'dp'), axis=0)  35.8 us
    all_gather x1, waiting for transfers between devices, on_device(): gathered = lax.all_gather(new_mom_weights, 'dp', axis=0, tiled=True)  30.3 us
    dot_general x4, matrix products, matmul(): return jnp.dot(left, right, preferred_element_type=jnp.float32)  26.6 us
    unnamed x109, local copies, waits for them, and re-layouts  16.3 us
    dot_general x4, matrix products, outer_sum(): lax.dot_general(left, right, (((0,), (0,)), ((), ())), preferred_element_...  14.2 us
  transfers between devices with their start and end apart: 3, of which 3 were waited for; matrix products, arithmetic and copies ran while one was open for 4% of the time, Pallas kernels for 0%

profile of v1, /device:TPU:21, one launch (start us, length us, event | category | flops | bytes accessed | tf_op | source)
XLA Modules:
  0.0 459.7 jit_solution(14399910342949501524)
XLA Ops:
  8.0 1.4 slice_bitcast_fusion.1
  9.4 1.3 convert_reduce_fusion.1
  10.8 1.5 fusion.17
  12.3 1.3 slice_bitcast_fusion
  13.6 57.5 %all-gather.3.cloned.1.call-done = bf16[13824,128]{1,0:T(8,128)(2,1)} async-done(((bf16[432,128]{1,0:T(8,128)(2,1)}), bf16[13824,128]{1,0:T(8,128)(2,1)}) %all-gather.3.cloned.1.call-update) | async-done | bytes 3538960 | tf_op jit(solution)/shard_map/all_gather | solution.py:175
  71.2 1.2 slice.95
  72.4 1.9 reshape.171
  74.3 2.7 fusion.7
  77.0 5.9 %reshape.182 = bf16[5,197,3,6,64]{4,3,2,1,0:T(8,128)(2,1)} reshape(bf16[985,1152]{1,0:T(8,128)(2,1)S(1)} %fusion.7) | data formatting | bytes 4538880 | tf_op jit(solution)/shard_map/reshape | solution.py:190
  82.9 5.8 %fusion.46 = (bf16[5,197,1,6,64]{4,3,2,1,0:T(8,128)(2,1)}, bf16[5,197,1,6,64]{4,3,2,1,0:T(8,128)(2,1)}, bf16[5,197,1,6,64]{4,3,2,1,0:T(8,128)(2,1)}) fusion(bf16[5,197,3,6,64]{4,3,2,1,0:T(8,128)(2,1)} %reshape.182), kind=kLoop, calls=%fused_computation.112 | loop fusion | bytes 4538880 | tf_op jit(solution)/shard_map/slice | solution.py:192
  88.7 3.5 copy.58
  92.3 3.7 copy.59
  98.3 1.5 copy-done
  99.7 3.4 copy.57
  103.1 4.4 fusion.20
  107.5 1.8 copy.41
  109.3 2.8 convert_element_type.81
  113.0 1.9 fusion.48
  115.4 1.6 fusion.47
  117.0 3.5 reshape.174
  120.5 3.1 reshape.175
  123.6 17.5 %multiply_convert_fusion.1 = (bf16[985,1536]{1,0:T(8,128)(2,1)}, f32[985,1536]{1,0:T(8,128)S(1)}, f32[985,1536]{1,0:T(8,128)S(1)}) fusion(f32[1536]{0:T(1024)S(1)} %copy-done.35, bf16[384,1536]{1,0:T(8,128)(2,1)} %reshape.174, f32[985,384]{1,0:T(8,128)S(1)} %get-tuple-element.43, f32[384]{0:T(512)S(1)} %copy-done.41, f32[384]{0:T(512)S(1)} %copy-done.32, ...), kind=kOutput, calls=%fused_computation.9 | convolution fusion | flops 1263699840 | bytes 17839304 | tf_op jit(solution)/shard_map/dot_general | solution.py:60
  141.1 4.2 convert_reduce_fusion
  145.3 2.6 multiply_reduce_fusion.2
  152.1 2.5 reshape.183
  154.6 4.0 copy.43
  158.6 5.2 %multiply_reduce_fusion = (f32[5,6,197]{2,1,0:T(8,128)S(1)}, f32[5,6,197,197]{2,3,1,0:T(8,128)S(1)}) fusion(f32[5,6,197,197]{2,3,1,0:T(8,128)} %copy-done, f32[5,6,197]{2,1,0:T(8,128)S(1)} %log_add_fusion, bf16[5,197,6,64]{1,3,2,0:T(8,128)(2,1)} %copy.43, bf16[5,197,1,6,64]{1,4,3,0,2:T(8,128)(2,1)} %copy-done.11), kind=kOutput, calls=%fused_computation.3 | convolution fusion | flops 153677728 | bytes 10874400 | tf_op jit(solution)/shard_map/bqhd,bkhd->bhqk/dot_general | solution.py:238
  163.9 2.1 multiply_convert_fusion
  168.4 1.2 convolution_bitcast_fusion
  170.7 3.0 fusion.40
  173.7 1.4 fusion.49
  175.8 4.5 copy.48
  180.3 7.6 %convert_element_type.91 = bf16[985,1152]{0,1:T(8,128)(2,1)} reshape(bf16[5,197,3,6,64]{1,0,4,3,2:T(8,128)(2,1)} %copy.48) | data formatting | bytes 4538880 | tf_op jit(solution)/shard_map/convert_element_type | solution.py:251
  187.9 2.7 reshape.179
  190.6 1.9 reshape.178
  192.6 4.6 fusion.36
  197.1 2.5 reshape.177
  199.6 5.3 %fusion.50 = f32[1536,384]{1,0:T(8,128)} fusion(bf16[985,1536]{1,0:T(8,128)(2,1)} %get-tuple-element.23, bf16[985,384]{1,0:T(8,128)(2,1)} %param.9), kind=kOutput, calls=%fused_computation.116 | convolution fusion | flops 1161953280 | bytes 6141696 | tf_op jit(solution)/shard_map/dot_general | solution.py:64
  204.9 3.2 reshape.180
  208.1 8.2 %maximum_bitcast_fusion = f32[13824,128]{1,0:T(8,128)} fusion(f32[589824]{0:T(1024)} %reshape.180, f32[589824]{0:T(1024)S(1)} %reshape.179, f32[147456]{0:T(1024)} %reshape.178, f32[442368]{0:T(1024)} %reshape.177), kind=kLoop, calls=%fused_computation.1 | loop fusion | flops 5308416 | bytes 14155776 | tf_op jit(solution)/shard_map/reshape | solution.py:263
  216.4 116.5 %reduce-scatter.2.cloned.1.call-done = f32[432,128]{1,0:T(8,128)} async-done(((f32[13824,128]{1,0:T(8,128)}), f32[432,128]{1,0:T(8,128)}) %reduce-scatter.2.cloned.1.call-update) | async-done | bytes 221200 | tf_op jit(solution)/shard_map/reduce_scatter | solution.py:278
  332.9 1.7 multiply_add_fusion
  334.6 3.0 fusion.42
  339.3 1.9 convert_reduce_fusion.2
  341.2 35.8 %all_gather.11 = f32[32,36,128]{2,1,0:T(8,128)S(1)} all-gather(f32[1,36,128]{2,1,0:T(8,128)S(1)} %bitcast.86), channel_id=1, replica_groups=mesh['dp'=32] {'dp'}, dimensions={0}, use_global_device_ids=true | all-gather | bytes 608256 | tf_op jit(solution)/shard_map/all_gather | solution.py:277
  377.7 4.5 add_convert_fusion.1
  382.2 30.3 %all-gather.5.cloned.1.call-done.mom_ref = f32[13824,128]{1,0:T(8,128)} async-done(((f32[432,128]{1,0:T(8,128)}), f32[13824,128]{1,0:T(8,128)}) %all-gather.5.cloned.1.call-update) | async-done | bytes 7077904 | tf_op jit(solution)/shard_map/all_gather | solution.py:280
  412.6 40.4 %polar.1 = f32[432,128]{1,0:T(8,128)} custom-call(f32[13824,128]{1,0:T(8,128)} %all-gather.5.cloned.1.call-done.mom_ref), custom_call_target="tpu_custom_call" | custom-call | tf_op jit(solution)/shard_map/polar/pallas_call | solution.py:156
  (141 shorter events, 15.0 us)
Async XLA Ops:
  7.2 67.2 %copy-start.1 = (bf16[985,384]{1,0:T(8,128)(2,1)S(1)}, bf16[985,384]{1,0:T(8,128)(2,1)}, u32[]{:S(2)}) copy-start(bf16[985,384]{1,0:T(8,128)(2,1)} %param.6) | copy-start | bytes 2269444
  7.2 64.0 %all-gather.3.cloned.1.call-start = ((), (), s32[]{:S(2)}) async-start(), calls=%async_computation.1 | async-start | bytes 3649536 | tf_op jit(solution)/shard_map/all_gather | solution.py:175
  7.9 325.0 %reduce-scatter.2.cloned.1.call-start = ((), (), s32[]{:S(2)}) async-start(), calls=%async_computation.2 | async-start | bytes 7299072 | tf_op jit(solution)/shard_map/reduce_scatter | solution.py:278
  9.4 67.6 %copy-start.28 = (f32[384]{0:T(512)}, f32[384]{0:T(512)S(1)}, u32[]{:S(2)}) copy-start(f32[384]{0:T(512)S(1)} %get-tuple-element.39) | copy-start | bytes 4612
  9.4 67.6 %copy-start.39 = (f32[384]{0:T(512)}, f32[384]{0:T(512)S(1)}, u32[]{:S(2)}) copy-start(f32[384]{0:T(512)S(1)} %get-tuple-element.38) | copy-start | bytes 4612
  92.3 4.8 %copy-start.7 = (bf16[5,197,1,6,64]{1,4,3,0,2:T(8,128)(2,1)}, bf16[5,197,1,6,64]{1,4,3,0,2:T(8,128)(2,1)S(1)}, u32[]{:S(2)}) copy-start(bf16[5,197,1,6,64]{1,4,3,0,2:T(8,128)(2,1)S(1)} %copy.58) | copy-start | bytes 2269444
  97.0 2.7 copy-start
  103.1 4.4 copy-start.11
  107.5 4.6 %slice-start.2 = ((bf16[13824,128]{1,0:T(8,128)(2,1)}), bf16[1152,128]{1,0:T(8,128)(2,1)S(1)}, s32[]{:S(2)}) async-start(bf16[13824,128]{1,0:T(8,128)(2,1)} %all-gather.3.cloned.1.call-done), calls=%async_computation.6 | async-start | bytes 589824 | tf_op jit(solution)/shard_map/slice | solution.py:33
  107.5 5.5 %copy-start.36 = (f32[384]{0:T(512)S(1)}, f32[384]{0:T(512)}, u32[]{:S(2)}) copy-start(f32[384]{0:T(512)} %get-tuple-element.35) | copy-start | bytes 4612
  113.0 2.4 copy-start.16
  114.9 32.9 %copy-start.2 = (f32[985,384]{1,0:T(8,128)}, f32[985,384]{1,0:T(8,128)S(1)}, u32[]{:S(2)}) copy-start(f32[985,384]{1,0:T(8,128)S(1)} %get-tuple-element.43) | copy-start | bytes 4538884
  115.0 32.9 %copy-start.25 = (f32[985]{0:T(1024)}, f32[985]{0:T(1024)S(1)}, u32[]{:S(2)}) copy-start(f32[985]{0:T(1024)S(1)} %broadcast_multiply_fusion.1) | copy-start | bytes 11824
  115.4 32.5 %copy-start.30 = (f32[985]{0:T(1024)}, f32[985]{0:T(1024)S(1)}, u32[]{:S(2)}) copy-start(f32[985]{0:T(1024)S(1)} %fusion.33) | copy-start | bytes 11824
  117.0 6.6 %copy-start.32 = (f32[384]{0:T(512)S(1)}, f32[384]{0:T(512)}, u32[]{:S(2)}) copy-start(f32[384]{0:T(512)} %get-tuple-element.34) | copy-start | bytes 4612
  117.0 6.6 %copy-start.35 = (f32[1536]{0:T(1024)S(1)}, f32[1536]{0:T(1024)}, u32[]{:S(2)}) copy-start(f32[1536]{0:T(1024)} %slice_bitcast_fusion) | copy-start | bytes 18436
  117.0 6.6 %copy-start.41 = (f32[384]{0:T(512)S(1)}, f32[384]{0:T(512)}, u32[]{:S(2)}) copy-start(f32[384]{0:T(512)} %get-tuple-element.33) | copy-start | bytes 4612
  123.6 17.5 %copy-start.17 = (bf16[985,384]{1,0:T(8,128)(2,1)S(1)}, bf16[985,384]{1,0:T(8,128)(2,1)}, u32[]{:S(2)}) copy-start(bf16[985,384]{1,0:T(8,128)(2,1)} %param.9) | copy-start | bytes 2269444
  123.6 17.5 %copy-start.20 = (bf16[1536,384]{1,0:T(8,128)(2,1)S(1)}, bf16[1536,384]{1,0:T(8,128)(2,1)}, u32[]{:S(2)}) copy-start(bf16[1536,384]{1,0:T(8,128)(2,1)} %reshape.175) | copy-start | bytes 3538948
  141.1 4.2 copy-start.22
  145.3 2.6 copy-start.45
  147.9 3.6 copy-start.19
  154.6 9.2 %slice-start = ((s8[6144000]{0:T(1024)(128)(4,1)}), s8[1949696]{0:T(1024)(128)(4,1)S(1)}, s32[]{:S(2)}) async-start(s8[6144000]{0:T(1024)(128)(4,1)} %bitcast.84), calls=%async_computation.4 | async-start | bytes 3899392
  158.6 5.2 %slice-start.1 = ((s8[6144000]{0:T(1024)(128)(4,1)}), s8[4194304]{0:T(1024)(128)(4,1)S(1)}, s32[]{:S(2)}) async-start(s8[6144000]{0:T(1024)(128)(4,1)} %bitcast.84), calls=%async_computation.5 | async-start | bytes 8388608
  163.9 2.1 copy-start.10
  168.3 1.4 copy-start.3
  168.3 1.4 copy-start.26
  168.4 1.4 copy-start.31
  168.4 1.4 copy-start.33
  168.4 1.4 copy-start.42
  168.4 2.4 copy-start.46
  170.7 3.0 copy-start.14
  187.9 4.7 %copy-start.29 = (f32[384]{0:T(512)S(1)}, f32[384]{0:T(512)}, u32[]{:S(2)}) copy-start(f32[384]{0:T(512)} %copy-done.28) | copy-start | bytes 4612
  187.9 4.7 %copy-start.40 = (f32[384]{0:T(512)S(1)}, f32[384]{0:T(512)}, u32[]{:S(2)}) copy-start(f32[384]{0:T(512)} %copy-done.39) | copy-start | bytes 4612
  216.3 116.6 %copy-start.23 = (f32[432,128]{1,0:T(8,128)S(1)}, f32[432,128]{1,0:T(8,128)}, u32[]{:S(2)}) copy-start(f32[432,128]{1,0:T(8,128)} %param.10) | copy-start | bytes 663556
  216.3 118.3 %copy-start.15 = (bf16[985,1152]{0,1:T(8,128)(2,1)S(1)}, bf16[985,1152]{0,1:T(8,128)(2,1)}, u32[]{:S(2)}) copy-start(bf16[985,1152]{0,1:T(8,128)(2,1)} %convert_element_type.91) | copy-start | bytes 6808324
  216.4 196.2 %all-gather.5.cloned.1.call-start = ((), (), s32[]{:S(2)}) async-start(), calls=%async_computation.3 | async-start | bytes 7299072 | tf_op jit(solution)/shard_map/all_gather | solution.py:280
  337.7 1.2 copy-start.37
  337.7 1.2 copy-start.44
  337.7 1.2 copy-start.43
  337.7 1.4 copy-start.6
  337.7 1.6 copy-start.18
  339.3 1.9 copy-start.34
  339.3 37.8 %copy-start.27 = (f32[36,128]{1,0:T(8,128)S(1)}, f32[36,128]{1,0:T(8,128)}, u32[]{:S(2)}) copy-start(f32[36,128]{1,0:T(8,128)} %param.11) | copy-start | bytes 55300
  339.3 38.4 %copy-start.4 = (f32[985,384]{1,0:T(8,128)S(1)}, f32[985,384]{1,0:T(8,128)}, u32[]{:S(2)}) copy-start(f32[985,384]{1,0:T(8,128)} %copy-done.2) | copy-start | bytes 4538884
  339.3 38.4 %copy-start.21 = (bf16[1536,384]{1,0:T(8,128)(2,1)S(1)}, bf16[1536,384]{1,0:T(8,128)(2,1)}, u32[]{:S(2)}) copy-start(bf16[1536,384]{1,0:T(8,128)(2,1)} %reshape.175) | copy-start | bytes 3538948
  339.3 38.4 %copy-start.38 = (f32[384]{0:T(512)S(1)}, f32[384]{0:T(512)}, u32[]{:S(2)}) copy-start(f32[384]{0:T(512)} %get-tuple-element.32) | copy-start | bytes 4612
  377.1 5.1 %copy-start.24 = (f32[36,128]{1,0:T(8,128)}, f32[36,128]{1,0:T(8,128)S(1)}, u32[]{:S(2)}) copy-start(f32[36,128]{1,0:T(8,128)S(1)} %reduce_sum.231) | copy-start | bytes 55300
  (5 other events, 5.5 us)
Sparse Core Ops, SparseCore 0:
  10.9 60.1 all-gather.2
  216.5 116.3 reduce-scatter.1
  336.8 75.6 all-gather.4

commit v2 on v1

--- a/solution.py
+++ b/solution.py
@@ -168,6 +168,59 @@
         compiler_params=pltpu.CompilerParams(vmem_limit_bytes=48 * 1024 * 1024),
         name="polar",
     )(mom)
+
+
+def exchange(value, bit, count):
+    return lax.ppermute(value, "dp", [(i, i ^ (1 << bit)) for i in range(count)])
+
+
+def bit_orders(count):
+    top = count.bit_length() - 2
+    order_a = list(range(top))
+    order_b = [0, 2, 1] + order_a[3:]
+    return top, order_a, order_b
+
+
+def scatter_sum(blocks, count):
+    index = lax.axis_index("dp")
+    top, order_a, order_b = bit_orders(count)
+    shape = blocks.shape[1:]
+    whole = blocks.reshape((2,) * (top + 1) + shape)
+    parts = [whole[0], whole[1]]
+    lives = [list(range(top - 1, -1, -1)) for _ in range(2)]
+    for bits in zip(order_a, order_b):
+        for which, bit in enumerate(bits):
+            axis = lives[which].index(bit)
+            mine = (index >> bit) & 1
+            keep = lax.dynamic_index_in_dim(parts[which], mine, axis, keepdims=False)
+            send = lax.dynamic_index_in_dim(parts[which], 1 - mine, axis, keepdims=False)
+            got = exchange(send.astype(jnp.bfloat16), bit, count)
+            parts[which] = keep.astype(jnp.float32) + got.astype(jnp.float32)
+            lives[which].remove(bit)
+    low_half = ((index >> top) & 1) == 0
+    keep = jnp.where(low_half, parts[0], parts[1])
+    send = jnp.where(low_half, parts[1], parts[0])
+    return keep + exchange(send.astype(jnp.bfloat16), top, count).astype(jnp.float32)
+
+
+def gather_blocks(block, count):
+    index = lax.axis_index("dp")
+    top, order_a, order_b = bit_orders(count)
+    got = exchange(block, top, count)
+    low_half = ((index >> top) & 1) == 0
+    parts = [jnp.where(low_half, block, got), jnp.where(low_half, got, block)]
+    lives = [[], []]
+    for bits in zip(order_a[::-1], order_b[::-1]):
+        for which, bit in enumerate(bits):
+            got = exchange(parts[which], bit, count)
+            live = sorted(lives[which] + [bit], reverse=True)
+            axis = live.index(bit)
+            is_low = ((index >> bit) & 1) == 0
+            first = jnp.where(is_low, parts[which], got)
+            second = jnp.where(is_low, got, parts[which])
+            parts[which] = jnp.stack([first, second], axis=axis)
+            lives[which] = live
+    return jnp.stack(parts).reshape((count * block.shape[0],) + block.shape[1:])
 
 
 def on_device(inputs, weights, vectors, cotangent, mom_weights, mom_vectors):
@@ -258,7 +311,10 @@
     d_input_norm, grad_ln1_gain, grad_ln1_shift = norm_pull(d_normed)
     grad_inputs = d_middle + d_input_norm
     local_grads = jnp.concatenate(
-        [grad_qkv.reshape(-1), grad_out.reshape(-1), grad_up.reshape(-1), grad_down.reshape(-1)]
+        [
+            item.astype(jnp.bfloat16).reshape(-1)
+            for item in (grad_qkv, grad_out, grad_up, grad_down)
+        ]
     )
     local_grads = local_grads.reshape(-1, 128)
     local_vector_grads = jnp.concatenate(
@@ -275,7 +331,12 @@
         ]
     ).reshape(-1, 128)
     grad_vectors = jnp.sum(lax.all_gather(local_vector_grads, "dp"), axis=0)
-    grad_weights = lax.psum_scatter(local_grads, "dp", scatter_dimension=0, tiled=True)
+    if count >= 8 and count & (count - 1) == 0:
+        grad_weights = scatter_sum(local_grads.reshape(count, -1, 128), count)
+    else:
+        grad_weights = lax.psum_scatter(
+            local_grads.astype(jnp.float32), "dp", scatter_dimension=0, tiled=True
+        )
     new_mom_weights = MOMENTUM * mom_weights + grad_weights
     gathered = lax.all_gather(new_mom_weights, "dp", axis=0, tiled=True)
     new_mom_vectors = MOMENTUM * mom_vectors + grad_vectors

time: 467 us -> 379 us (0.81)
  waiting for transfers between devices: 205 us -> 105 us
  starting transfers between devices: 0.12 us -> 7.96 us
    reduce_scatter x1 -> x0, waiting for transfers between devices: 117 us -> none  [on_device(): lax.psum_scatter(local_grads, 'dp', scatter_dimension=0, tiled=True)]
    ppermute x0 -> x9, waiting for transfers between devices: none -> 19.1 us  [exchange(): return lax.ppermute(value, 'dp', [(i, i ^ 1 << bit) for i in range(count)])]
    reshape x1 -> x0, other arithmetic: 8.22 us -> none  [on_device(): local_grads = local_grads.reshape(-1, 128)]
    ppermute x0 -> x9, starting transfers between devices: none -> 7.88 us  [exchange(): return lax.ppermute(value, 'dp', [(i, i ^ 1 << bit) for i in range(count)])]
    add x0 -> x6, other arithmetic: none -> 5.53 us  [scatter_sum(): parts[which] = keep.astype(jnp.float32) + got.astype(jnp.float32)]
    unnamed x109 -> x93, local copies, waits for them, and re-layouts: 16.3 us -> 16.9 us
  transfers between devices with their start and end apart: 3 -> 11, of which waited for: 3 -> 10; matrix products, arithmetic and copies ran while one was open for 4% -> 7% of each run, Pallas kernels for 0% -> 0%
where the time goes in v2:
time: 379 us; the launch traced here: 372 us
  waiting for transfers between devices  105 us (28%)
  local copies, waits for them, and re-layouts  79.1 us (21%)
  matrix products  63.9 us (17%)
  Pallas kernels  40.1 us (11%)
  blocking collectives  38.8 us (10%)
  other arithmetic  21.7 us (6%)
  between operations  15 us (4%)
  starting transfers between devices  7.96 us (2%)
    all_gather x1, waiting for transfers between devices, on_device(): whole = lax.all_gather(weights, 'dp', axis=0, tiled=True)  57.5 us
    pallas_call x1, Pallas kernels, polar_update(): pl.pallas_call(functools.partial(polar_kernel, rows), out_shape=jax.Shape...  40.1 us
    all_gather x1, blocking collectives, on_device(): grad_vectors = jnp.sum(lax.all_gather(local_vector_grads, 'dp'), axis=0)  38.8 us
    all_gather x1, waiting for transfers between devices, on_device(): gathered = lax.all_gather(new_mom_weights, 'dp', axis=0, tiled=True)  27.7 us
    dot_general x4, matrix products, matmul(): return jnp.dot(left, right, preferred_element_type=jnp.float32)  27.2 us
    ppermute x9, waiting for transfers between devices, exchange(): return lax.ppermute(value, 'dp', [(i, i ^ 1 << bit) for i in range(count)])  19.1 us
    unnamed x93, local copies, waits for them, and re-layouts  16.9 us
    convert_element_type x2, local copies, waits for them, and re-layouts, on_device(): d_qkv = jnp.stack([grad_queries, grad_keys, grad_values], axis=2).astype(...  12.5 us
  transfers between devices with their start and end apart: 11, of which 10 were waited for; matrix products, arithmetic and copies ran while one was open for 7% of the time, Pallas kernels for 0%

profile of v2, /device:TPU:21, one launch (start us, length us, event | category | flops | bytes accessed | tf_op | source)
XLA Modules:
  0.0 371.6 jit_solution(10642068962319422159)
XLA Ops:
  8.0 1.4 slice_bitcast_fusion.1
  10.8 1.6 fusion.17
  13.7 57.5 %all-gather.3.cloned.1.call-done = bf16[13824,128]{1,0:T(8,128)(2,1)} async-done(((bf16[432,128]{1,0:T(8,128)(2,1)}), bf16[13824,128]{1,0:T(8,128)(2,1)}) %all-gather.3.cloned.1.call-update) | async-done | bytes 3538960 | tf_op jit(solution)/shard_map/all_gather | solution.py:228
  72.3 1.9 reshape.182
  74.2 2.7 fusion.7
  76.9 5.9 %reshape.194 = bf16[5,197,3,6,64]{4,3,2,1,0:T(8,128)(2,1)} reshape(bf16[985,1152]{1,0:T(8,128)(2,1)S(1)} %fusion.7) | data formatting | bytes 4538880 | tf_op jit(solution)/shard_map/reshape | solution.py:243
  82.8 5.8 %fusion.50 = (bf16[5,197,1,6,64]{4,3,2,1,0:T(8,128)(2,1)}, bf16[5,197,1,6,64]{4,3,2,1,0:T(8,128)(2,1)}, bf16[5,197,1,6,64]{4,3,2,1,0:T(8,128)(2,1)}) fusion(bf16[5,197,3,6,64]{4,3,2,1,0:T(8,128)(2,1)} %reshape.194), kind=kLoop, calls=%fused_computation.146 | loop fusion | bytes 4538880 | tf_op jit(solution)/shard_map/slice | solution.py:245
  88.7 3.6 copy.66
  92.3 3.7 copy.67
  99.7 3.4 copy.65
  103.1 4.4 %fusion.20 = bf16[5,197,6,64]{1,3,2,0:T(8,128)(2,1)S(1)} fusion(bf16[5,197,1,6,64]{1,4,3,0,2:T(8,128)(2,1)S(1)} %copy.65, f32[5,6,197,197]{2,3,1,0:T(8,128)} %copy-done, f32[5,6,197]{2,1,0:T(8,128)S(1)} %log_add_fusion), kind=kOutput, calls=%fused_computation.68 | convolution fusion | flops 152897616 | bytes 6193680 | tf_op jit(solution)/shard_map/bhqk,bkhd->bqhd/dot_general | solution.py:255
  108.1 2.1 convert_element_type.171
  112.1 2.2 fusion.52
  115.8 3.5 reshape.185
  119.3 1.4 reshape.186
  120.7 17.6 %multiply_convert_fusion.1 = (bf16[985,1536]{1,0:T(8,128)(2,1)}, f32[985,1536]{1,0:T(8,128)S(1)}, f32[985,1536]{1,0:T(8,128)S(1)}) fusion(f32[1536]{0:T(1024)S(1)} %copy-done.33, bf16[384,1536]{1,0:T(8,128)(2,1)} %reshape.185, f32[985,384]{1,0:T(8,128)S(1)} %get-tuple-element.51, f32[384]{0:T(512)S(1)} %get-tuple-element.41, f32[384]{0:T(512)S(1)} %get-tuple-element.42, ...), kind=kOutput, calls=%fused_computation.8 | convolution fusion | flops 1263699840 | bytes 17839304 | tf_op jit(solution)/shard_map/dot_general | solution.py:60
  138.2 4.2 %convert_reduce_fusion = (f32[1536]{0:T(1024)}, bf16[985,1536]{1,0:T(8,128)(2,1)S(1)}) fusion(f32[985,1536]{1,0:T(8,128)S(1)} %get-tuple-element.26, bf16[985,384]{1,0:T(8,128)(2,1)S(1)} %copy-done.20, bf16[1536,384]{1,0:T(8,128)(2,1)S(1)} %copy-done.27, f32[985,1536]{1,0:T(8,128)S(1)} %get-tuple-element.52, f32[1536]{0:T(1024)S(1)} %copy-done.33), kind=kOutput, calls=%fused_computation.6 | convolution fusion | flops 1187672064 | bytes 17078016 | tf_op jit(solution)/shard_map/dot_general | solution.py:70
  142.4 2.6 multiply_reduce_fusion.2
  148.6 2.4 reshape.195
  151.0 4.0 %copy.47 = bf16[5,197,6,64]{1,3,2,0:T(8,128)(2,1)} copy(bf16[5,197,6,64]{3,2,1,0:T(8,128)(2,1)} %reshape.195) | data formatting | bytes 1512960 | tf_op jit(solution)/shard_map/reshape | solution.py:280
  155.0 5.2 %multiply_reduce_fusion = (f32[5,6,197]{2,1,0:T(8,128)S(1)}, f32[5,6,197,197]{2,3,1,0:T(8,128)S(1)}) fusion(f32[5,6,197,197]{2,3,1,0:T(8,128)} %copy-done, f32[5,6,197]{2,1,0:T(8,128)S(1)} %log_add_fusion, bf16[5,197,6,64]{1,3,2,0:T(8,128)(2,1)} %copy.47, bf16[5,197,1,6,64]{1,4,3,0,2:T(8,128)(2,1)} %copy-done.9), kind=kOutput, calls=%fused_computation.2 | convolution fusion | flops 153677728 | bytes 10874400 | tf_op jit(solution)/shard_map/bqhd,bkhd->bhqk/dot_general | solution.py:291
  160.2 1.4 multiply_convert_fusion
  166.0 1.5 convolution_convert_fusion.2
  169.6 4.5 %copy.52 = bf16[5,197,3,6,64]{1,0,4,3,2:T(8,128)(2,1)} copy(bf16[5,197,3,6,64]{1,4,3,0,2:T(8,128)(2,1)S(1)} %maximum_convert_fusion) | data formatting | bytes 4538880 | tf_op jit(solution)/shard_map/convert_element_type | solution.py:304
  174.1 8.0 %convert_element_type.181 = bf16[985,1152]{0,1:T(8,128)(2,1)} reshape(bf16[5,197,3,6,64]{1,0,4,3,2:T(8,128)(2,1)} %copy.52) | data formatting | bytes 4538880 | tf_op jit(solution)/shard_map/convert_element_type | solution.py:304
  182.1 2.4 reshape.190
  184.5 1.8 reshape.189
  186.3 4.2 %convolution_convert_fusion = bf16[384,1152]{1,0:T(8,128)(2,1)} fusion(bf16[985,1152]{0,1:T(8,128)(2,1)} %convert_element_type.181, bf16[985,384]{1,0:T(8,128)(2,1)S(1)} %copy-done.2, f32[384]{0:T(512)S(1)} %copy-done.36, f32[384]{0:T(512)S(1)} %get-tuple-element.47, f32[985]{0:T(1024)S(1)} %fusion.38, f32[985]{0:T(1024)S(1)} %broadcast_multiply_fusion.2), kind=kOutput, calls=%fused_computation.27 | convolution fusion | flops 874176768 | bytes 3921608 | tf_op jit(solution)/shard_map/dot_general | solution.py:64
  190.6 2.8 reshape.188
  193.4 4.7 %convolution_convert_fusion.1 = bf16[1536,384]{1,0:T(8,128)(2,1)} fusion(bf16[985,1536]{1,0:T(8,128)(2,1)} %get-tuple-element.25, bf16[985,384]{1,0:T(8,128)(2,1)S(1)} %copy-done.21), kind=kOutput, calls=%fused_computation.28 | convolution fusion | flops 1162543104 | bytes 4962048 | tf_op jit(solution)/shard_map/dot_general | solution.py:64
  198.1 3.2 reshape.191
  201.3 1.8 pad_maximum_fusion
  208.0 1.6 convert_add_fusion.2
  210.8 1.4 convert_add_fusion.3
  215.4 7.0 %collective-permute-done.5 = bf16[2,2,432,128]{3,2,0,1:T(8,128)(2,1)} collective-permute-done((bf16[2,2,432,128]{3,2,0,1:T(8,128)(2,1)}, bf16[2,2,432,128]{3,2,0,1:T(8,128)(2,1)}, u32[]{:S(2)}, u32[]{:S(2)}) %collective-permute-start.5) | collective-permute-done | bytes 442400 | tf_op jit(solution)/shard_map/ppermute | solution.py:174
  222.4 1.4 bitcast_add_fusion
  224.2 1.6 collective-permute-done.1
  228.2 1.6 collective-permute-done.6
  233.9 3.5 collective-permute-done.3
  238.4 1.6 collective-permute-start.8
  240.0 3.0 collective-permute-done.8
  243.0 1.8 multiply_add_fusion
  244.9 3.9 %fusion.46 = (f32[384]{0:T(512)S(1)}, f32[985]{0:T(1024)S(1)}, f32[985,384]{1,0:T(8,128)S(1)}) fusion(f32[384]{0:T(512)S(1)} %get-tuple-element.47, f32[985]{0:T(1024)S(1)} %broadcast_multiply_fusion.2, bf16[985,384]{1,0:T(8,128)(2,1)S(1)} %copy-done.2, bf16[985,1152]{0,1:T(8,128)(2,1)} %convert_element_type.181, bf16[384,1152]{1,0:T(8,128)(2,1)} %reshape.182), kind=kOutput, calls=%fused_computation.144 | convolution fusion | flops 873733056 | bytes 5434568 | tf_op jit(solution)/shard_map/dot_general | solution.py:70
  250.3 2.0 convert_reduce_fusion.2
  252.4 38.8 %all_gather.11 = f32[32,36,128]{2,1,0:T(8,128)S(1)} all-gather(f32[1,36,128]{2,1,0:T(8,128)S(1)} %bitcast.138), channel_id=1, replica_groups=mesh['dp'=32] {'dp'}, dimensions={0}, use_global_device_ids=true | all-gather | bytes 608256 | tf_op jit(solution)/shard_map/all_gather | solution.py:333
  291.9 4.8 %add_convert_fusion.1 = bf16[985,384]{1,0:T(8,128)(2,1)} fusion(f32[985,384]{1,0:T(8,128)S(1)} %get-tuple-element.51, bf16[985,1536]{1,0:T(8,128)(2,1)} %get-tuple-element.25, bf16[1536,384]{1,0:T(8,128)(2,1)} %reshape.186, f32[384]{0:T(512)S(1)} %copy-done.34), kind=kOutput, calls=%fused_computation.63 | convolution fusion | flops 1163088000 | bytes 6476544 | tf_op jit(solution)/shard_map/dot_general | solution.py:60
  296.7 27.7 %all-gather.5.cloned.1.call-done.mom_ref = f32[13824,128]{1,0:T(8,128)} async-done(((f32[432,128]{1,0:T(8,128)}), f32[13824,128]{1,0:T(8,128)}) %all-gather.5.cloned.1.call-update) | async-done | bytes 7077904 | tf_op jit(solution)/shard_map/all_gather | solution.py:341
  324.4 40.1 %polar.1 = f32[432,128]{1,0:T(8,128)} custom-call(f32[13824,128]{1,0:T(8,128)} %all-gather.5.cloned.1.call-done.mom_ref), custom_call_target="tpu_custom_call" | custom-call | tf_op jit(solution)/shard_map/polar/pallas_call | solution.py:156
  (156 shorter events, 41.5 us)
Async XLA Ops:
  7.2 64.0 %all-gather.3.cloned.1.call-start = ((), (), s32[]{:S(2)}) async-start(), calls=%async_computation | async-start | bytes 3649536 | tf_op jit(solution)/shard_map/all_gather | solution.py:228
  7.9 316.5 %all-gather.5.cloned.1.call-start = ((), (), s32[]{:S(2)}) async-start(), calls=%async_computation.1 | async-start | bytes 7299072 | tf_op jit(solution)/shard_map/all_gather | solution.py:341
  9.4 64.9 %copy-start.35 = (f32[384]{0:T(512)}, f32[384]{0:T(512)S(1)}, u32[]{:S(2)}) copy-start(f32[384]{0:T(512)S(1)} %get-tuple-element.46) | copy-start | bytes 4612
  10.7 63.5 %copy-start.1 = (bf16[985,384]{1,0:T(8,128)(2,1)S(1)}, bf16[985,384]{1,0:T(8,128)(2,1)}, u32[]{:S(2)}) copy-start(bf16[985,384]{1,0:T(8,128)(2,1)} %param.6) | copy-start | bytes 2269444
  92.3 4.8 %copy-start.5 = (bf16[5,197,1,6,64]{1,4,3,0,2:T(8,128)(2,1)}, bf16[5,197,1,6,64]{1,4,3,0,2:T(8,128)(2,1)S(1)}, u32[]{:S(2)}) copy-start(bf16[5,197,1,6,64]{1,4,3,0,2:T(8,128)(2,1)S(1)} %copy.66) | copy-start | bytes 2269444
  97.1 2.6 copy-start
  103.1 9.0 %copy-start.9 = (bf16[5,197,1,6,64]{1,4,3,0,2:T(8,128)(2,1)}, bf16[5,197,1,6,64]{1,4,3,0,2:T(8,128)(2,1)S(1)}, u32[]{:S(2)}) copy-start(bf16[5,197,1,6,64]{1,4,3,0,2:T(8,128)(2,1)S(1)} %copy.65) | copy-start | bytes 2269444
  112.1 2.6 copy-start.16
  115.8 4.9 %copy-start.33 = (f32[1536]{0:T(1024)S(1)}, f32[1536]{0:T(1024)}, u32[]{:S(2)}) copy-start(f32[1536]{0:T(1024)} %slice_bitcast_fusion) | copy-start | bytes 18436
  120.6 17.6 %copy-start.20 = (bf16[985,384]{1,0:T(8,128)(2,1)S(1)}, bf16[985,384]{1,0:T(8,128)(2,1)}, u32[]{:S(2)}) copy-start(bf16[985,384]{1,0:T(8,128)(2,1)} %param.9) | copy-start | bytes 2269444
  120.6 17.6 %copy-start.27 = (bf16[1536,384]{1,0:T(8,128)(2,1)S(1)}, bf16[1536,384]{1,0:T(8,128)(2,1)}, u32[]{:S(2)}) copy-start(bf16[1536,384]{1,0:T(8,128)(2,1)} %reshape.186) | copy-start | bytes 3538948
  138.2 4.2 %copy-start.28 = (bf16[384,1536]{1,0:T(8,128)(2,1)S(1)}, bf16[384,1536]{1,0:T(8,128)(2,1)}, u32[]{:S(2)}) copy-start(bf16[384,1536]{1,0:T(8,128)(2,1)} %reshape.185) | copy-start | bytes 3538948
  142.4 2.6 copy-start.18
  145.6 2.3 copy-start.25
  151.0 9.2 %slice-start = ((s8[6144000]{0:T(1024)(128)(4,1)}), s8[1949696]{0:T(1024)(128)(4,1)S(1)}, s32[]{:S(2)}) async-start(s8[6144000]{0:T(1024)(128)(4,1)} %bitcast.134), calls=%async_computation.2 | async-start | bytes 3899392
  155.0 5.2 %slice-start.1 = ((s8[6144000]{0:T(1024)(128)(4,1)}), s8[4194304]{0:T(1024)(128)(4,1)S(1)}, s32[]{:S(2)}) async-start(s8[6144000]{0:T(1024)(128)(4,1)} %bitcast.134), calls=%async_computation.3 | async-start | bytes 8388608
  160.2 1.5 copy-start.8
  161.7 1.2 copy-start.6
  164.1 1.9 copy-start.19
  166.0 1.6 copy-start.17
  166.0 1.6 copy-start.24
  182.1 4.3 %copy-start.2 = (bf16[985,384]{1,0:T(8,128)(2,1)S(1)}, bf16[985,384]{1,0:T(8,128)(2,1)}, u32[]{:S(2)}) copy-start(bf16[985,384]{1,0:T(8,128)(2,1)} %param.6) | copy-start | bytes 2269444
  182.1 4.3 %copy-start.36 = (f32[384]{0:T(512)S(1)}, f32[384]{0:T(512)}, u32[]{:S(2)}) copy-start(f32[384]{0:T(512)} %copy-done.35) | copy-start | bytes 4612
  186.3 7.0 %copy-start.21 = (bf16[985,384]{1,0:T(8,128)(2,1)S(1)}, bf16[985,384]{1,0:T(8,128)(2,1)}, u32[]{:S(2)}) copy-start(bf16[985,384]{1,0:T(8,128)(2,1)} %param.9) | copy-start | bytes 2269444
  198.1 3.2 copy-start.15
  205.2 2.8 collective-permute-start.4
  206.5 4.3 %collective-permute-start = (bf16[2,2,2,432,128]{4,3,0,1,2:T(8,128)(2,1)}, bf16[2,2,2,432,128]{4,3,0,1,2:T(8,128)(2,1)}, u32[]{:S(2)}, u32[]{:S(2)}) collective-permute-start(bf16[2,2,2,432,128]{4,3,0,1,2:T(8,128)(2,1)} %bitcast.133), channel_id=1, source_target_pairs={{0,1},{1,0},{2,3},{3,2},{4,5},{5,4},{6,7},{7,6},{8,9},{9,8},{10,11... | collective-permute-start | bytes 2654216 | tf_op jit(solution)/shard_map/ppermute | solution.py:174
  209.6 4.6 %copy-start.12 = (f32[2,2,2,432,128]{4,3,0,2,1:T(8,128)}, f32[2,2,2,432,128]{4,3,0,2,1:T(8,128)S(1)}, u32[]{:S(2)}) copy-start(f32[2,2,2,432,128]{4,3,0,2,1:T(8,128)S(1)} %convert_add_fusion.2) | copy-start | bytes 5308420
  210.6 11.8 %collective-permute-start.5 = (bf16[2,2,432,128]{3,2,0,1:T(8,128)(2,1)}, bf16[2,2,432,128]{3,2,0,1:T(8,128)(2,1)}, u32[]{:S(2)}, u32[]{:S(2)}) collective-permute-start(bf16[2,2,432,128]{3,2,0,1:T(8,128)(2,1)} %fusion.31), channel_id=1, source_target_pairs={{0,4},{1,5},{2,6},{3,7},{4,0},{5,1},{6,2},{7,3},{8,12},{9,13},{10,... | collective-permute-start | bytes 1327112 | tf_op jit(solution)/shard_map/ppermute | solution.py:174
  212.2 1.2 copy-start.13
  214.2 11.5 %collective-permute-start.1 = (bf16[2,2,432,128]{3,2,0,1:T(8,128)(2,1)}, bf16[2,2,432,128]{3,2,0,1:T(8,128)(2,1)}, u32[]{:S(2)}, u32[]{:S(2)}) collective-permute-start(bf16[2,2,432,128]{3,2,0,1:T(8,128)(2,1)} %fusion.30), channel_id=1, source_target_pairs={{0,2},{1,3},{2,0},{3,1},{4,6},{5,7},{6,4},{7,5},{8,10},{9,11},{10,... | collective-permute-start | bytes 1327112 | tf_op jit(solution)/shard_map/ppermute | solution.py:174
  215.4 10.4 %copy-start.14 = (f32[2,2,2,432,128]{4,3,0,1,2:T(8,128)S(1)}, f32[2,2,2,432,128]{4,3,0,1,2:T(8,128)}, u32[]{:S(2)}) copy-start(f32[2,2,2,432,128]{4,3,0,1,2:T(8,128)} %copy-done.13) | copy-start | bytes 5308420
  223.8 6.0 %collective-permute-start.6 = (bf16[2,432,128]{2,1,0:T(8,128)(2,1)S(1)}, bf16[2,432,128]{2,1,0:T(8,128)(2,1)S(1)}, u32[]{:S(2)}, u32[]{:S(2)}) collective-permute-start(bf16[2,432,128]{2,1,0:T(8,128)(2,1)S(1)} %fusion.35), channel_id=1, source_target_pairs={{0,2},{1,3},{2,0},{3,1},{4,6},{5,7},{6,4},{7,5},{8,10},{9,11},{10,... | collective-permute-start | bytes 663560 | tf_op jit(solution)/shard_map/ppermute | solution.py:174
  226.9 16.2 %copy-start.29 = (f32[432,128]{1,0:T(8,128)S(1)}, f32[432,128]{1,0:T(8,128)}, u32[]{:S(2)}) copy-start(f32[432,128]{1,0:T(8,128)} %param.10) | copy-start | bytes 663556
  226.9 5.3 %collective-permute-start.2 = (bf16[2,432,128]{2,1,0:T(8,128)(2,1)S(1)}, bf16[2,432,128]{2,1,0:T(8,128)(2,1)S(1)}, u32[]{:S(2)}, u32[]{:S(2)}) collective-permute-start(bf16[2,432,128]{2,1,0:T(8,128)(2,1)S(1)} %fusion.34), channel_id=1, source_target_pairs={{0,4},{1,5},{2,6},{3,7},{4,0},{5,1},{6,2},{7,3},{8,12},{9,13},{10,... | collective-permute-start | bytes 663560 | tf_op jit(solution)/shard_map/ppermute | solution.py:174
  229.9 2.4 copy-start.26
  229.9 4.0 %collective-permute-start.7 = (bf16[432,128]{1,0:T(8,128)(2,1)S(1)}, bf16[432,128]{1,0:T(8,128)(2,1)S(1)}, u32[]{:S(2)}, u32[]{:S(2)}) collective-permute-start(bf16[432,128]{1,0:T(8,128)(2,1)S(1)} %fusion.37), channel_id=1, source_target_pairs={{0,8},{1,9},{2,10},{3,11},{4,12},{5,13},{6,14},{7,15},{8,0},{9,1},... | collective-permute-start | bytes 331784 | tf_op jit(solution)/shard_map/ppermute | solution.py:174
  232.3 5.1 %collective-permute-start.3 = (bf16[432,128]{1,0:T(8,128)(2,1)S(1)}, bf16[432,128]{1,0:T(8,128)(2,1)S(1)}, u32[]{:S(2)}, u32[]{:S(2)}) collective-permute-start(bf16[432,128]{1,0:T(8,128)(2,1)S(1)} %fusion.36), channel_id=1, source_target_pairs={{0,8},{1,9},{2,10},{3,11},{4,12},{5,13},{6,14},{7,15},{8,0},{9,1},... | collective-permute-start | bytes 331784 | tf_op jit(solution)/shard_map/ppermute | solution.py:174
  238.4 4.7 %collective-permute-start.8 = (bf16[432,128]{1,0:T(8,128)(2,1)S(1)}, bf16[432,128]{1,0:T(8,128)(2,1)S(1)}, u32[]{:S(2)}, u32[]{:S(2)}) collective-permute-start(bf16[432,128]{1,0:T(8,128)(2,1)S(1)} %select_convert_fusion), channel_id=1, source_target_pairs={{0,16},{1,17},{2,18},{3,19},{4,20},{5,21},{6,22},{7,23},{8,24},{9,... | collective-permute-start | bytes 331784 | tf_op jit(solution)/shard_map/ppermute | solution.py:174
  244.9 4.8 %copy-start.11 = (bf16[985,1152]{0,1:T(8,128)(2,1)S(1)}, bf16[985,1152]{0,1:T(8,128)(2,1)}, u32[]{:S(2)}) copy-start(bf16[985,1152]{0,1:T(8,128)(2,1)} %convert_element_type.181) | copy-start | bytes 6808324
  248.7 1.2 copy-start.38
  248.7 1.3 copy-start.37
  248.7 1.4 copy-start.4
  248.8 1.6 copy-start.22
  250.3 2.0 copy-start.32
  250.3 40.9 %copy-start.31 = (f32[36,128]{1,0:T(8,128)S(1)}, f32[36,128]{1,0:T(8,128)}, u32[]{:S(2)}) copy-start(f32[36,128]{1,0:T(8,128)} %param.11) | copy-start | bytes 55300
  250.3 41.6 %copy-start.34 = (f32[384]{0:T(512)S(1)}, f32[384]{0:T(512)}, u32[]{:S(2)}) copy-start(f32[384]{0:T(512)} %get-tuple-element.40) | copy-start | bytes 4612
  291.3 5.5 %copy-start.30 = (f32[36,128]{1,0:T(8,128)}, f32[36,128]{1,0:T(8,128)S(1)}, u32[]{:S(2)}) copy-start(f32[36,128]{1,0:T(8,128)S(1)} %reduce_sum.231) | copy-start | bytes 55300
  (5 other events, 5.4 us)
Sparse Core Ops, SparseCore 0:
  10.9 60.1 all-gather.2
  245.0 79.3 all-gather.4
